TPU v7x, 128 devices: a whole 4x4x4 slice. The times are simulated.
128 devices in a mesh: row: 8 (over y, core), col: 16 (over z, x).
Axes of the slice: x: 4, y: 4, z: 4, core: 2. Of those that a mesh axis runs over, the one named last changes fastest.
Arguments:
- integrals: bfloat16 [1024, 512, 256], P('row', 'col'), may hold values from -0.625 to 0.625
- virt_green: bfloat16 [512, 512], P('col'), may hold values from -0.375 to 0.375
- occ_green: bfloat16 [512, 512], P('col'), may hold values from -0.375 to 0.375
- block_list: int32 [16, 8], replicated, may hold values from 0 to 15, as said below
- block_owner: int32 [16], replicated, may hold values from 0 to 15, each once
- block_sizes: int32 [16], replicated, may hold values from 16 to 32
Outputs:
- response: float32 [1024, 1024], P('row', 'col')
Inputs may be any that keep to these rules, and one draw needn't show every extreme that they name: `block_list`: each row names 8 different atoms.
All inputs are finite; a program needn't handle non-finite values.
Results may differ from a plain program's by a relative error of at most 0.0041.
Values may be sent and summed in bfloat16 or wider, within the bound.
A program may use at most 128 MiB of HBM per device.

v0:
```python
import jax
import jax.numpy as jnp
from jax import lax
from jax.sharding import PartitionSpec as P


def slot_atoms(block_owner, count):
    ids = jnp.arange(count, dtype=jnp.int32)
    match = block_owner[:, None] == ids[None, :]
    return jnp.sum(jnp.where(match, ids[:, None], 0), axis=0)


def shards(integrals, virt_green, occ_green, block_list, block_owner, block_sizes):
    count = block_owner.shape[0]
    slots = integrals.shape[1]
    aux_rows = integrals.shape[0]
    virt_full, occ_full = (
        lax.all_gather(virt_green, "col", axis=0, tiled=True),
        lax.all_gather(occ_green, "col", axis=0, tiled=True),
    )
    atoms = slot_atoms(block_owner, count)
    sizes = block_sizes[atoms]
    valid = (jnp.arange(slots, dtype=jnp.int32)[None, :] < sizes[:, None]).reshape(count * slots)
    both = valid[:, None] & valid[None, :]
    virt_eff = jnp.where(both, virt_full, jnp.zeros_like(virt_full))
    occ_eff = jnp.where(both, occ_full, jnp.zeros_like(occ_full))
    mine = atoms[lax.axis_index("col")]
    owners = block_owner[block_list[mine]]
    row_index = (owners[:, None] * slots + jnp.arange(slots, dtype=jnp.int32)[None, :]).reshape(-1)
    virt_rows = jnp.take(virt_eff, row_index, axis=0)
    occ_rows = jnp.take(occ_eff, row_index, axis=0)
    flat = integrals.reshape(aux_rows * slots, integrals.shape[2])
    left = jnp.dot(flat, virt_rows, preferred_element_type=jnp.float32).astype(jnp.bfloat16)
    left = left.reshape(aux_rows, slots, -1)
    right = jnp.einsum(
        "qsl,lm->qms", integrals, occ_rows, preferred_element_type=jnp.float32
    ).astype(jnp.bfloat16)
    right_local = lax.all_to_all(right, "col", split_axis=1, concat_axis=2, tiled=True)
    left_share, right_share = (
        lax.all_to_all(left, "row", split_axis=2, concat_axis=0, tiled=True),
        lax.all_to_all(right_local, "row", split_axis=2, concat_axis=0, tiled=True),
    )
    total = lax.dot_general(
        left_share.reshape(left_share.shape[0], -1),
        right_share.reshape(right_share.shape[0], -1),
        (((1,), (1,)), ((), ())),
        preferred_element_type=jnp.float32,
    )
    columns = lax.psum_scatter(total, "col", scatter_dimension=1, tiled=True)
    columns = lax.psum_scatter(columns, "row", scatter_dimension=0, tiled=True)
    return columns


def solution(mesh):
    in_specs = (P("row", "col", None), P("col", None), P("col", None), P(), P(), P())
    out_specs = P("row", "col")
    return jax.shard_map(shards, mesh=mesh, in_specs=in_specs, out_specs=out_specs, check_vma=False)
```

profile of v0, /device:TPU:1, one launch (start us, length us, event | category | flops | bytes accessed | tf_op | source)
XLA Modules:
  0.0 354.5 jit_solution(13616506063608094692)
XLA Ops:
  10.9 1.3 gather_fusion.1
  12.4 1.3 gather_fusion
  13.9 21.0 %all_gather.6 = bf16[512,512]{1,0:T(8,128)(2,1)S(1)} all-gather(bf16[32,512]{1,0:T(8,128)(2,1)} %param.9), channel_id=1, replica_groups=mesh['row'=8,'col'=16] {'col'}, dimensions={0}, use_global_device_ids=true | all-gather | bytes 557056 | tf_op jit(solution)/shard_map/all_gather | solution.py:18
  34.8 17.5 %all_gather.7 = bf16[512,512]{1,0:T(8,128)(2,1)S(1)} all-gather(bf16[32,512]{1,0:T(8,128)(2,1)} %param.10), channel_id=1, replica_groups=mesh['row'=8,'col'=16] {'col'}, dimensions={0}, use_global_device_ids=true | all-gather | bytes 557056 | tf_op jit(solution)/shard_map/all_gather | solution.py:19
  52.7 1.2 gather_fusion.3
  53.9 3.4 convert_bitcast_fusion
  57.2 4.7 %copy.60 = bf16[128,512,32]{0,2,1:T(8,128)(2,1)} copy(bf16[128,512,32]{0,1,2:T(8,128)(2,1)S(1)} %convert_bitcast_fusion) | data formatting | bytes 8388608 | tf_op jit(solution)/shard_map/convert_element_type | solution.py:37
  61.9 5.1 %all-to-all-start.1 = ((bf16[128,512,32]{0,2,1:T(8,128)(2,1)}), bf16[128,512,32]{0,2,1:T(8,128)(2,1)}, u32[]{:S(2)}, u32[]{:S(2)}) async-start(bf16[128,512,32]{0,2,1:T(8,128)(2,1)} %copy.60), calls=%async_computation.1 | async-start | bytes 8388608 | tf_op jit(solution)/shard_map/all_to_all | solution.py:38
  67.0 1.2 gather_fusion.2
  68.1 3.3 fusion
  71.5 6.5 %copy.54 = bf16[4096,512]{1,0:T(8,128)(2,1)} copy(bf16[4096,512]{0,1:T(8,128)(2,1)} %fusion) | data formatting | bytes 8388608 | tf_op jit(solution)/shard_map/convert_element_type | solution.py:33
  78.0 9.1 %copy.55 = bf16[128,32,512]{0,1,2:T(8,128)(2,1)} copy(bf16[128,32,512]{2,1,0:T(8,128)(2,1)} %bitcast.44) | data formatting | bytes 8388608 | tf_op jit(solution)/shard_map/reshape | solution.py:34
  87.1 26.3 %all-to-all-done.1 = bf16[128,512,32]{0,2,1:T(8,128)(2,1)} async-done(((bf16[128,512,32]{0,2,1:T(8,128)(2,1)}), bf16[128,512,32]{0,2,1:T(8,128)(2,1)}, u32[]{:S(2)}, u32[]{:S(2)}) %all-to-all-start.1) | async-done | bytes 4194336 | tf_op jit(solution)/shard_map/all_to_all | solution.py:38
  113.4 16.6 %all-to-all-start = ((bf16[128,32,512]{0,1,2:T(8,128)(2,1)}), bf16[128,32,512]{0,1,2:T(8,128)(2,1)}, u32[]{:S(2)}, u32[]{:S(2)}) async-start(bf16[128,32,512]{0,1,2:T(8,128)(2,1)} %copy.55), calls=%async_computation | async-start | bytes 8388608 | tf_op jit(solution)/shard_map/all_to_all | solution.py:40
  130.0 3.4 copy.61
  133.4 4.6 %copy.62 = bf16[128,32,512]{0,1,2:T(8,128)(2,1)} copy(bf16[128,32,512]{0,2,1:T(8,128)(2,1)S(1)} %bitcast.45) | data formatting | bytes 8388608 | tf_op jit(solution)/shard_map/all_to_all | solution.py:38
  138.1 40.8 %all-to-all-done = bf16[128,32,512]{0,1,2:T(8,128)(2,1)} async-done(((bf16[128,32,512]{0,1,2:T(8,128)(2,1)}), bf16[128,32,512]{0,1,2:T(8,128)(2,1)}, u32[]{:S(2)}, u32[]{:S(2)}) %all-to-all-start) | async-done | bytes 4194336 | tf_op jit(solution)/shard_map/all_to_all | solution.py:40
  178.9 5.3 %all-to-all-start.2 = ((bf16[128,32,512]{0,1,2:T(8,128)(2,1)}), bf16[128,32,512]{0,1,2:T(8,128)(2,1)}, u32[]{:S(2)}, u32[]{:S(2)}) async-start(bf16[128,32,512]{0,1,2:T(8,128)(2,1)} %copy.62), calls=%async_computation.2 | async-start | bytes 8388608 | tf_op jit(solution)/shard_map/all_to_all | solution.py:41
  184.2 6.8 %copy.57 = bf16[8,128,32,64]{1,0,3,2:T(8,128)(2,1)} copy(bf16[8,128,32,64]{1,2,3,0:T(8,128)(2,1)} %bitcast.9) | data formatting | bytes 8388608 | tf_op jit(solution)/shard_map/all_to_all | solution.py:40
  191.1 42.1 %all-to-all-done.2 = bf16[128,32,512]{0,1,2:T(8,128)(2,1)} async-done(((bf16[128,32,512]{0,1,2:T(8,128)(2,1)}), bf16[128,32,512]{0,1,2:T(8,128)(2,1)}, u32[]{:S(2)}, u32[]{:S(2)}) %all-to-all-start.2) | async-done | bytes 4194336 | tf_op jit(solution)/shard_map/all_to_all | solution.py:41
  233.2 5.0 %copy.64 = bf16[8,128,32,64]{1,0,3,2:T(8,128)(2,1)S(1)} copy(bf16[8,128,32,64]{1,2,3,0:T(8,128)(2,1)} %bitcast.17) | data formatting | bytes 8388608 | tf_op jit(solution)/shard_map/all_to_all | solution.py:41
  238.2 6.1 %fusion.1 = f32[1024,1024]{0,1:T(8,128)} fusion(bf16[256,8,8,128]{3,2,1,0:T(8,128)(2,1)S(1)} %bitcast.47, bf16[256,8,8,128]{3,2,1,0:T(8,128)(2,1)S(1)} %bitcast.46), kind=kOutput, calls=%fused_computation.6 | convolution fusion | flops 4294967296 | bytes 12582912 | tf_op jit(solution)/shard_map/dot_general | solution.py:43
  244.4 72.0 %reduce-scatter.3.cloned.1.call-done = f32[1024,64]{0,1:T(8,128)} async-done(((f32[1024,1024]{0,1:T(8,128)}), f32[1024,64]{0,1:T(8,128)}) %reduce-scatter.3.cloned.1.call-update) | async-done | bytes 262160 | tf_op jit(solution)/shard_map/reduce_scatter | solution.py:49
  316.4 31.2 %reduce-scatter.5.cloned.1.call-done = f32[128,64]{0,1:T(8,128)} async-done(((f32[1024,64]{0,1:T(8,128)}), f32[128,64]{0,1:T(8,128)}) %reduce-scatter.5.cloned.1.call-update) | async-done | bytes 32784 | tf_op jit(solution)/shard_map/reduce_scatter | solution.py:50
  (24 shorter events, 3.1 us)
Async XLA Ops:
  6.5 47.3 %copy-start = (bf16[128,32,256]{2,1,0:T(8,128)(2,1)S(1)}, bf16[128,32,256]{2,1,0:T(8,128)(2,1)}, u32[]{:S(2)}) copy-start(bf16[128,32,256]{2,1,0:T(8,128)(2,1)} %param.8) | copy-start | bytes 6291460
  61.9 51.5 %all-to-all-start.1 = ((bf16[128,512,32]{0,2,1:T(8,128)(2,1)}), bf16[128,512,32]{0,2,1:T(8,128)(2,1)}, u32[]{:S(2)}, u32[]{:S(2)}) async-start(bf16[128,512,32]{0,2,1:T(8,128)(2,1)} %copy.60), calls=%async_computation.1 | async-start | bytes 8388608 | tf_op jit(solution)/shard_map/all_to_all | solution.py:38
  113.4 65.5 %all-to-all-start = ((bf16[128,32,512]{0,1,2:T(8,128)(2,1)}), bf16[128,32,512]{0,1,2:T(8,128)(2,1)}, u32[]{:S(2)}, u32[]{:S(2)}) async-start(bf16[128,32,512]{0,1,2:T(8,128)(2,1)} %copy.55), calls=%async_computation | async-start | bytes 8388608 | tf_op jit(solution)/shard_map/all_to_all | solution.py:40
  178.9 54.3 %all-to-all-start.2 = ((bf16[128,32,512]{0,1,2:T(8,128)(2,1)}), bf16[128,32,512]{0,1,2:T(8,128)(2,1)}, u32[]{:S(2)}, u32[]{:S(2)}) async-start(bf16[128,32,512]{0,1,2:T(8,128)(2,1)} %copy.62), calls=%async_computation.2 | async-start | bytes 8388608 | tf_op jit(solution)/shard_map/all_to_all | solution.py:41
  184.2 132.2 %reduce-scatter.3.cloned.1.call-start = ((), (), s32[]{:S(2)}) async-start(), calls=%async_computation.5 | async-start | bytes 4456448 | tf_op jit(solution)/shard_map/reduce_scatter | solution.py:49
  233.2 5.0 %copy-start.1 = (bf16[8,128,32,64]{1,0,3,2:T(8,128)(2,1)S(1)}, bf16[8,128,32,64]{1,0,3,2:T(8,128)(2,1)}, u32[]{:S(2)}) copy-start(bf16[8,128,32,64]{1,0,3,2:T(8,128)(2,1)} %copy.57) | copy-start | bytes 12582916
  244.3 103.3 %reduce-scatter.5.cloned.1.call-start = ((), (), s32[]{:S(2)}) async-start(), calls=%async_computation.6 | async-start | bytes 294912 | tf_op jit(solution)/shard_map/reduce_scatter | solution.py:50
Sparse Core Ops, SparseCore 0:
  244.4 71.9 reduce-scatter.2
  318.9 28.6 reduce-scatter.4
where the time goes:
time: 357 us; the launch traced here: 354 us
  waiting for transfers between devices  212 us (59%)
  local copies, waits for them, and re-layouts  46.8 us (13%)
  blocking collectives  38.5 us (11%)
  starting transfers between devices  27 us (8%)
  between operations  15.4 us (4%)
  matrix products  12.8 us (4%)
    reduce_scatter x1, waiting for transfers between devices, shards(): columns = lax.psum_scatter(total, 'col', scatter_dimension=1, tiled=True)  72 us
    all_to_all x1, waiting for transfers between devices, shards(): lax.all_to_all(right_local, 'row', split_axis=2, concat_axis=0, tiled=True)  42.1 us
    all_to_all x1, waiting for transfers between devices, shards(): lax.all_to_all(left, 'row', split_axis=2, concat_axis=0, tiled=True)  40.8 us
    reduce_scatter x1, waiting for transfers between devices, shards(): columns = lax.psum_scatter(columns, 'row', scatter_dimension=0, tiled=True)  31.2 us
    all_to_all x1, waiting for transfers between devices, shards(): lax.all_to_all(right, 'col', split_axis=1, concat_axis=2, tiled=True)  26.3 us
    all_gather x1, blocking collectives, shards(): lax.all_gather(virt_green, 'col', axis=0, tiled=True)  21 us
    all_gather x1, blocking collectives, shards(): lax.all_gather(occ_green, 'col', axis=0, tiled=True)  17.5 us
    all_to_all x1, starting transfers between devices, shards(): lax.all_to_all(left, 'row', split_axis=2, concat_axis=0, tiled=True)  16.6 us
  transfers between devices with their start and end apart: 5, of which 5 were waited for; matrix products, arithmetic and copies ran while one was open for 10% of the time, Pallas kernels for 0%

commit v1 on v0

v1 whole, which is shorter than its diff:
```python
import jax
import jax.numpy as jnp
from jax import lax
from jax.experimental import pallas as pl
from jax.experimental.pallas import tpu as pltpu
from jax.sharding import PartitionSpec as P

BF = jnp.bfloat16
F32 = jnp.float32
ANY = pl.BlockSpec(memory_space=pl.ANY)
VMEM = pl.BlockSpec(memory_space=pltpu.VMEM)
SMEM = pl.BlockSpec(memory_space=pltpu.SMEM)
ROWS, COLS, YS = 8, 16, 4


def place():
    r = lax.axis_index("row")
    c = lax.axis_index("col")
    return r, c, r // 2, r % 2


def loop(lo, hi, body):
    def step(i, carry):
        body(i)
        return carry

    lax.fori_loop(lo, hi, step, 0)


def remote(src, dst, ssem, rsem, row, col):
    return pltpu.make_async_remote_copy(
        src_ref=src, dst_ref=dst, send_sem=ssem, recv_sem=rsem,
        device_id=(row, col), device_id_type=pl.DeviceIdType.MESH,
    )


def spread_kernel(ints, virt, occ, vall, oall, mine, quart,
                  vs, vr, os_, or_, ms, mr, qs, qr, fs, fr, loc):
    r, c, y, core = place()

    def green(src, dst, s, q, k):
        to = (c + k) % COLS
        return remote(src, dst.at[pl.ds(c * 32, 32)], s.at[k], q.at[k], r, to)

    def block(k):
        to = (c + k) % COLS
        return remote(ints.at[pl.ds(to * 8, 8)], mine.at[c], ms.at[k], mr.at[k], r, to)

    def piece(yy):
        return ints.at[:, pl.ds((yy // 2) * 16, 16), pl.ds((yy % 2) * 128, 128)]

    def quarter(k):
        to = (y + k) % YS
        return remote(piece(to), quart.at[r], qs.at[k], qr.at[k], to * 2 + core, c)

    def forward(k):
        frm = ((y + YS - k) % YS) * 2 + core
        return remote(quart.at[frm], quart.at[frm], fs.at[k], fr.at[k], y * 2 + (1 - core), c)

    def own(k):
        return remote(piece(y), quart.at[r], fs.at[0], fr.at[0], y * 2 + (1 - core), c)

    loop(1, COLS, lambda k: (green(virt, vall, vs, vr, k).start(), green(occ, oall, os_, or_, k).start()))
    loop(1, YS, lambda k: quarter(k).start())
    loop(1, COLS, lambda k: block(k).start())
    copies = [
        pltpu.make_async_copy(virt, vall.at[pl.ds(c * 32, 32)], loc.at[0]),
        pltpu.make_async_copy(occ, oall.at[pl.ds(c * 32, 32)], loc.at[1]),
        pltpu.make_async_copy(ints.at[pl.ds(c * 8, 8)], mine.at[c], loc.at[2]),
        pltpu.make_async_copy(piece(y), quart.at[r], loc.at[3]),
    ]
    for copy in copies:
        copy.start()
    own(0).start()

    def pass_on(k):
        quarter(k).wait_recv()
        forward(k).start()

    loop(1, YS, pass_on)
    for copy in copies:
        copy.wait()
    loop(1, COLS, lambda k: (green(virt, vall, vs, vr, k).wait(), green(occ, oall, os_, or_, k).wait()))
    loop(1, COLS, lambda k: block(k).wait())
    loop(1, YS, lambda k: quarter(k).wait_send())
    loop(1, YS, lambda k: forward(k).wait())
    own(0).wait()


def spread(ints, virt, occ):
    dma = pltpu.SemaphoreType.DMA
    return pl.pallas_call(
        spread_kernel,
        out_shape=(
            jax.ShapeDtypeStruct((512, 512), BF),
            jax.ShapeDtypeStruct((512, 512), BF),
            jax.ShapeDtypeStruct((16, 8, 32, 256), BF),
            jax.ShapeDtypeStruct((8, 128, 16, 128), BF),
        ),
        in_specs=[ANY] * 3,
        out_specs=(ANY,) * 4,
        scratch_shapes=[dma((16,))] * 6 + [dma((4,))] * 4 + [dma((4,))],
        compiler_params=pltpu.CompilerParams(has_side_effects=True),
    )(ints, virt, occ)


def factor_kernel(lists, owner, sizes, mine, virt, occ, out, atom, veff, oeff, left, left_t):
    for a in range(16):
        atom[owner[a]] = a
    lane = lax.broadcasted_iota(jnp.int32, (32, 512), 1)
    row = lax.broadcasted_iota(jnp.int32, (32, 512), 0)
    limit = jnp.zeros((32, 512), jnp.int32)
    for s in range(16):
        limit = jnp.where(lane // 32 == s, sizes[atom[s]], limit)
    inside = lane % 32 < limit
    for s in range(16):
        both = jnp.logical_and(inside, row < sizes[atom[s]])
        rows = pl.ds(s * 32, 32)
        veff[rows, :] = jnp.where(both, virt[rows, :], jnp.zeros((), BF))
        oeff[rows, :] = jnp.where(both, occ[rows, :], jnp.zeros((), BF))

    def listed(ref, s):
        a = atom[s]
        parts = [ref[pl.ds(pl.multiple_of(owner[lists[a, k]] * 32, 32), 32), :] for k in range(8)]
        return jnp.concatenate(parts, axis=0)

    def make_left(s):
        lhs = mine[s].reshape(256, 256)
        res = jnp.dot(lhs, listed(veff, s), preferred_element_type=F32).astype(BF)
        left[:, pl.ds(pl.multiple_of(s * 32, 32), 32), :] = res.reshape(8, 32, 512)

    loop(0, 16, make_left)

    def turn(p):
        left_t[p] = left[p].T

    loop(0, 8, turn)

    def make_out(t):
        lhs = left_t[:, pl.ds(pl.multiple_of(t * 32, 32), 32), :].reshape(256, 512)
        res = lax.dot_general(lhs, listed(oeff, t), (((1,), (1,)), ((), ())), preferred_element_type=F32)
        out[t] = res.astype(BF).reshape(8, 32, 256)

    loop(0, 16, make_out)


def factors(lists, owner, sizes, mine, virt, occ):
    return pl.pallas_call(
        factor_kernel,
        out_shape=jax.ShapeDtypeStruct((16, 8, 32, 256), BF),
        in_specs=[SMEM] * 3 + [VMEM] * 3,
        out_specs=VMEM,
        scratch_shapes=[
            pltpu.SMEM((16,), jnp.int32),
            pltpu.VMEM((512, 512), BF),
            pltpu.VMEM((512, 512), BF),
            pltpu.VMEM((8, 512, 512), BF),
            pltpu.VMEM((8, 512, 512), BF),
        ],
        compiler_params=pltpu.CompilerParams(vmem_limit_bytes=40 << 20),
    )(lists, owner, sizes, mine, virt, occ)


def finish_kernel(w, quart, out, wgot, qv, i2, w2, part, got, ws, wr, ps, pr, loc):
    r, c, y, core = place()
    me = y * COLS + c

    def send_w(k):
        to = (me + k) % 64
        yy, cc = to // COLS, to % COLS
        src = w.at[cc, :, pl.ds((yy // 2) * 16, 16), pl.ds((yy % 2) * 128, 128)]
        return remote(src, wgot.at[me], ws.at[k], wr.at[k], yy * 2 + core, cc)

    def send_part(k):
        to = (me + k) % 64
        yy, cc = to // COLS, to % COLS
        src = part.at[cc, :, pl.ds(pl.multiple_of(yy * 128, 128), 128)]
        return remote(src, got.at[me], ps.at[k], pr.at[k], yy * 2 + core, cc)

    loop(1, 64, lambda k: send_w(k).start())
    own = pltpu.make_async_copy(
        w.at[c, :, pl.ds((y // 2) * 16, 16), pl.ds((y % 2) * 128, 128)], wgot.at[me], loc.at[0])
    own.start()
    load = pltpu.make_async_copy(quart, qv, loc.at[1])
    load.start()
    a = lax.broadcasted_iota(jnp.int32, (256, 256), 0)
    b = lax.broadcasted_iota(jnp.int32, (256, 256), 1)
    perm = jnp.where((a // 16 == b % 16) & (a % 16 == b // 16), 1.0, 0.0).astype(BF)
    load.wait()

    def spread_rows(x, dst, at):
        x = jnp.dot(perm, x, preferred_element_type=F32).astype(BF)
        for j in range(16):
            dst[pl.ds(at, 16), j * 128:(j + 1) * 128] = x[j * 16:(j + 1) * 16, :]

    def lay_i(i):
        x = qv[i // 8, pl.ds(pl.multiple_of(i % 8 * 16, 16), 16)].reshape(256, 128)
        spread_rows(x, i2, pl.multiple_of(i * 16, 16))

    loop(0, 64, lay_i)
    loop(1, 64, lambda k: send_w(k).wait())
    own.wait()

    def lay_w(i):
        x = wgot[pl.ds(i * 2, 2)].reshape(256, 128)
        spread_rows(x, w2, pl.multiple_of(i * 16, 16))

    loop(0, 32, lay_w)

    def multiply(i):
        x = i2[pl.ds(pl.multiple_of(i * 256, 256), 256), :]
        res = lax.dot_general(x, w2[...], (((1,), (1,)), ((), ())), preferred_element_type=F32)
        part[pl.ds(i * 4, 4)] = res.astype(BF).reshape(4, 64, 512)

    loop(0, 4, multiply)
    loop(1, 64, lambda k: send_part(k).start())
    keep = pltpu.make_async_copy(
        part.at[c, :, pl.ds(pl.multiple_of(y * 128, 128), 128)], got.at[me], loc.at[2])
    keep.start()
    loop(1, 64, lambda k: send_part(k).wait())
    keep.wait()
    total = lax.fori_loop(0, 64, lambda i, acc: acc + got[i].astype(F32), jnp.zeros((64, 128), F32))
    out[...] = total.T


def finish(w, quart):
    dma = pltpu.SemaphoreType.DMA
    return pl.pallas_call(
        finish_kernel,
        out_shape=jax.ShapeDtypeStruct((128, 64), F32),
        in_specs=[ANY] * 2,
        out_specs=VMEM,
        scratch_shapes=[
            pltpu.VMEM((64, 8, 16, 128), BF),
            pltpu.VMEM((8, 128, 16, 128), BF),
            pltpu.VMEM((1024, 2048), BF),
            pltpu.VMEM((512, 2048), BF),
            pltpu.VMEM((16, 64, 512), BF),
            pltpu.VMEM((64, 64, 128), BF),
        ] + [dma((64,))] * 4 + [dma((3,))],
        compiler_params=pltpu.CompilerParams(has_side_effects=True, vmem_limit_bytes=40 << 20),
    )(w, quart)


def shards(integrals, virt_green, occ_green, block_list, block_owner, block_sizes):
    vall, oall, mine, quart = spread(integrals, virt_green, occ_green)
    w = factors(block_list, block_owner, block_sizes, mine, vall, oall)
    return finish(w, quart)


def solution(mesh):
    in_specs = (P("row", "col", None), P("col", None), P("col", None), P(), P(), P())
    return jax.shard_map(shards, mesh=mesh, in_specs=in_specs, out_specs=P("row", "col"), check_vma=False)
```

time: 357 us -> 142 us (0.40)
  waiting for transfers between devices: 212 us -> 0 us
  Pallas kernels: 0 us -> 137 us
  local copies, waits for them, and re-layouts: 46.8 us -> 5.16 us
  blocking collectives: 38.5 us -> 0 us
  starting transfers between devices: 27 us -> 0 us
  between operations: 15.4 us -> 0.06 us
  matrix products: 12.8 us -> 0 us
    pallas_call x0 -> x3, Pallas kernels: none -> 137 us  [the longest x1 66.5 us: finish(): pl.pallas_call(finish_kernel, out_shape=jax.ShapeDtypeStruct((128, 64), F...]
    all_to_all x3 -> x0, waiting for transfers between devices: 109 us -> none  [the longest x1 42.1 us: shards(): lax.all_to_all(right_local, 'row', split_axis=2, concat_axis=0, tiled=True)]
    reduce_scatter x2 -> x0, waiting for transfers between devices: 103 us -> none  [the longest x1 72 us: shards(): columns = lax.psum_scatter(total, 'col', scatter_dimension=1, tiled=True)]
    all_gather x2 -> x0, blocking collectives: 38.5 us -> none  [the longest x1 21 us: shards(): lax.all_gather(virt_green, 'col', axis=0, tiled=True)]
    all_to_all x3 -> x0, starting transfers between devices: 27 us -> none  [the longest x1 16.6 us: shards(): lax.all_to_all(left, 'row', split_axis=2, concat_axis=0, tiled=True)]
    all_to_all x4 -> x0, local copies, waits for them, and re-layouts: 19.9 us -> none  [the longest x2 8.08 us: shards(): lax.all_to_all(right, 'col', split_axis=1, concat_axis=2, tiled=True)]
    dot_general x3 -> x0, matrix products: 12.8 us -> none  [the longest x1 6.1 us: shards(): lax.dot_general(left_share.reshape(left_share.shape[0], -1), right_share....]
    convert_element_type x2 -> x0, local copies, waits for them, and re-layouts: 11.2 us -> none  [the longest x1 6.49 us: shards(): jnp.dot(flat, virt_rows, preferred_element_type=jnp.float32)]
  transfers between devices with their start and end apart: 5 -> 0, of which waited for: 5 -> 0; matrix products, arithmetic and copies ran while one was open for 10% -> 0% of each run, Pallas kernels for 0% -> 0%
where the time goes in v1:
time: 142 us
  Pallas kernels  137 us (96%)
  local copies, waits for them, and re-layouts  5.16 us (4%)
    pallas_call x1, Pallas kernels, finish(): pl.pallas_call(finish_kernel, out_shape=jax.ShapeDtypeStruct((128, 64), F...  66.5 us
    pallas_call x1, Pallas kernels, spread(): pl.pallas_call(spread_kernel, out_shape=(jax.ShapeDtypeStruct((512, 512),...  59.7 us
    pallas_call x1, Pallas kernels, factors(): pl.pallas_call(factor_kernel, out_shape=jax.ShapeDtypeStruct((16, 8, 32,...  10.5 us
    unnamed x13, local copies, waits for them, and re-layouts  4.46 us

profile of v1, /device:TPU:1, one launch (start us, length us, event | category | flops | bytes accessed | tf_op | source)
XLA Modules:
  0.0 141.8 jit_solution(17529199353949177560)
XLA Ops:
  0.0 0.0 copy-start.5
  0.0 0.0 copy-start.4
  0.0 0.8 copy.7.lists
  0.8 59.7 %shard_map.64 = (bf16[512,512]{1,0:T(8,128)(2,1)}, bf16[512,512]{1,0:T(8,128)(2,1)}, bf16[16,8,32,256]{3,2,1,0:T(8,128)(2,1)}, bf16[8,128,16,128]{3,2,1,0:T(8,128)(2,1)}) custom-call(bf16[128,32,256]{2,1,0:T(8,128)(2,1)} %ints.1, bf16[32,512]{1,0:T(8,128)(2,1)} %virt.1, bf16[32,512]{1,0:T(8,128)(2,1)} %occ.1), custom_call_target="tpu_custom_call" | custom-call | tf_op jit(solution)/shard_map/pallas_call | solution.py:92
  60.5 0.0 copy-done.5
  60.5 0.0 copy-done.4
  60.5 0.0 copy-start.1
  60.5 1.6 %copy-done.1 = bf16[16,8,32,256]{3,2,1,0:T(8,128)(2,1)S(1)} copy-done((bf16[16,8,32,256]{3,2,1,0:T(8,128)(2,1)S(1)}, bf16[16,8,32,256]{3,2,1,0:T(8,128)(2,1)}, u32[]{:S(2)}) %copy-start.1) | copy-done | bytes 2097176
  62.1 0.0 copy-start.2
  62.1 1.0 copy-done.2
  63.1 0.0 copy-start.3
  63.1 1.0 copy-done.3
  64.2 0.0 copy-start
  64.2 10.5 %shard_map.65.w = bf16[16,8,32,256]{3,2,1,0:T(8,128)(2,1)S(1)} custom-call(s32[16,8]{1,0:T(8,128)S(1)} %copy.7.lists, s32[16]{0:T(128)S(1)} %copy-done.4, s32[16]{0:T(128)S(1)} %copy-done.5, bf16[16,8,32,256]{3,2,1,0:T(8,128)(2,1)S(1)} %copy-done.1, bf16[512,512]{1,0:T(8,128)(2,1)S(1)} %copy-done.2, bf16[512,512]{1,0:T(8,128)(2,1)S(1)} %copy-done.3), custom_call_target="tpu_custom_call" | custom-call | tf_op jit(solution)/shard_map/pallas_call | solution.py:148
  74.6 0.0 copy-done
  74.6 66.5 %shard_map.66 = f32[128,64]{1,0:T(8,128)S(1)} custom-call(bf16[16,8,32,256]{3,2,1,0:T(8,128)(2,1)S(1)} %shard_map.65.w, bf16[8,128,16,128]{3,2,1,0:T(8,128)(2,1)S(1)} %copy-done), custom_call_target="tpu_custom_call" | custom-call | tf_op jit(solution)/shard_map/pallas_call | solution.py:228
  141.1 0.7 copy.8
Async XLA Ops:
  0.0 60.5 %copy-start.5 = (s32[16]{0:T(128)S(1)}, s32[16]{0:T(128)}, u32[]{:S(2)}) copy-start(s32[16]{0:T(128)} %sizes.1) | copy-start | bytes 196
  0.0 60.5 %copy-start.4 = (s32[16]{0:T(128)S(1)}, s32[16]{0:T(128)}, u32[]{:S(2)}) copy-start(s32[16]{0:T(128)} %owner.1) | copy-start | bytes 196
  60.5 1.6 %copy-start.1 = (bf16[16,8,32,256]{3,2,1,0:T(8,128)(2,1)S(1)}, bf16[16,8,32,256]{3,2,1,0:T(8,128)(2,1)}, u32[]{:S(2)}) copy-start(bf16[16,8,32,256]{3,2,1,0:T(8,128)(2,1)} %get-tuple-element.9.mine) | copy-start | bytes 6291460
  62.1 1.0 copy-start.2
  63.1 1.0 copy-start.3
  64.2 10.5 %copy-start = (bf16[8,128,16,128]{3,2,1,0:T(8,128)(2,1)S(1)}, bf16[8,128,16,128]{3,2,1,0:T(8,128)(2,1)}, u32[]{:S(2)}) copy-start(bf16[8,128,16,128]{3,2,1,0:T(8,128)(2,1)} %get-tuple-element.12.quart) | copy-start | bytes 12582916

commit v2 on v0

v2 whole, which is shorter than its diff:
```python
import jax
import jax.numpy as jnp
from jax import lax
from jax.experimental import pallas as pl
from jax.experimental.pallas import tpu as pltpu
from jax.sharding import PartitionSpec as P

BF = jnp.bfloat16
F32 = jnp.float32
ANY = pl.BlockSpec(memory_space=pl.ANY)
VMEM = pl.BlockSpec(memory_space=pltpu.VMEM)
SMEM = pl.BlockSpec(memory_space=pltpu.SMEM)
MESH = pl.DeviceIdType.MESH
NT = (((1,), (1,)), ((), ()))
ORDER = (10, 15, 4, 9, 14, 3, 8, 13, 2, 7, 12, 1, 6, 11, 5)


def loop(lo, hi, body, unroll=1):
    def step(i, carry):
        body(i)
        return carry

    lax.fori_loop(lo, hi, step, 0, unroll=unroll)


def remote(src, dst, ssem, rsem, row, col):
    return pltpu.make_async_remote_copy(
        src_ref=src, dst_ref=dst, send_sem=ssem, recv_sem=rsem, device_id=(row, col), device_id_type=MESH,
    )


def arrived(ref, sem):
    pltpu.make_async_copy(ref, ref, sem).wait()


def kernel(lists, owner, sizes, ints, virt, occ, out,
           starts, slot_size, gsrc, green, mine, quart, veff, oeff, left, left_t, wout, wgot, i2, w2, part, got,
           g1s, g1r, g2s, g2r, g3s, g3r, ms, mr, qs, qr, fs, fr, ws, wr, ps, pr, loc):
    r = lax.axis_index("row")
    c = lax.axis_index("col")
    y, core = r // 2, r % 2
    z, x = c // 4, c % 4
    me = y * 16 + c
    twin = y * 2 + (1 - core)

    def col_to(k):
        return (z + k // 4) % 4 * 4 + (x + k % 4) % 4

    def col_from(k):
        return (z + 4 - k // 4) % 4 * 4 + (x + 4 - k % 4) % 4

    def row_to(k):
        return (y + k) % 4 * 2 + core

    def piece(yy):
        return ints.at[:, pl.ds((yy // 2) * 16, 16), pl.ds((yy % 2) * 128, 128)]

    def green1(k):
        src = gsrc.at[core, :, pl.ds(pl.multiple_of(y * 128, 128), 128)]
        return remote(src, green.at[core, y, pl.ds(c * 32, 32)], g1s.at[k], g1r.at[k], r, col_to(k))

    def green2(k):
        return remote(green.at[core, y], green.at[core, y], g2s.at[k], g2r.at[k], row_to(k), c)

    def green3(k):
        q = (y + 4 - k) % 4
        return remote(green.at[core, q], green.at[core, q], g3s.at[k], g3r.at[k], twin, c)

    def block(k):
        return remote(ints.at[pl.ds(col_to(k) * 8, 8)], mine.at[c], ms.at[k], mr.at[k], r, col_to(k))

    def quarter(k):
        return remote(piece((y + k) % 4), quart.at[r], qs.at[k], qr.at[k], row_to(k), c)

    def forward(k):
        frm = (y + 4 - k) % 4 * 2 + core
        return remote(quart.at[frm], quart.at[frm], fs.at[k], fr.at[k], twin, c)

    def send_own():
        return remote(piece(y), quart.at[r], fs.at[0], fr.at[0], twin, c)

    def send_w(k):
        yy, cc = (y + k // 16) % 4, col_to(k % 16)
        src = wout.at[cc, :, pl.ds((yy // 2) * 16, 16), pl.ds((yy % 2) * 128, 128)]
        return remote(src, wgot.at[me], ws.at[k], wr.at[k], yy * 2 + core, cc)

    def send_part(k):
        yy, cc = (y + k // 16) % 4, col_to(k % 16)
        src = part.at[cc, :, pl.ds(pl.multiple_of(yy * 128, 128), 128)]
        return remote(src, got.at[me], ps.at[k], pr.at[k], yy * 2 + core, cc)

    own = [
        pltpu.make_async_copy(virt, gsrc.at[0], loc.at[0]),
        pltpu.make_async_copy(occ, gsrc.at[1], loc.at[1]),
        pltpu.make_async_copy(ints.at[pl.ds(c * 8, 8)], mine.at[c], mr.at[0]),
        pltpu.make_async_copy(piece(y), quart.at[r], qr.at[0]),
    ]
    for copy in own:
        copy.start()

    barrier = pltpu.get_barrier_semaphore()

    def greet(row, col):
        pl.semaphore_signal(barrier, inc=1, device_id=(row, col), device_id_type=MESH)

    loop(1, 16, lambda k: greet(r, col_to(k)))
    loop(1, 4, lambda k: greet(row_to(k), c))
    greet(twin, c)
    pl.semaphore_wait(barrier, 19)

    own[0].wait()
    own[1].wait()
    keep = pltpu.make_async_copy(
        gsrc.at[core, :, pl.ds(pl.multiple_of(y * 128, 128), 128)], green.at[core, y, pl.ds(c * 32, 32)], g1r.at[0])
    keep.start()
    for k in ORDER:
        green1(k).start()
    for k in (2, 1, 3):
        quarter(k).start()
    for k in ORDER:
        block(k).start()
    send_own().start()

    for s in range(16):
        atom = jnp.int32(0)
        for a in range(16):
            atom = jnp.where(owner[a] == s, a, atom)
        slot_size[s] = sizes[atom]
        for k in range(8):
            starts[s * 8 + k] = owner[lists[atom, k]]

    keep.wait()
    loop(1, 16, lambda k: green1(k).wait_recv())
    loop(1, 4, lambda k: green2(k).start())
    green3(0).start()

    def pass_green(k):
        green2(k).wait_recv()
        green3(k).start()

    loop(1, 4, pass_green)
    loop(0, 4, lambda k: green3(k).wait_recv())

    lane = lax.broadcasted_iota(jnp.int32, (32, 128), 1)
    row = lax.broadcasted_iota(jnp.int32, (32, 128), 0)
    for q in range(4):
        limit = jnp.zeros((32, 128), jnp.int32)
        for s in range(4):
            limit = jnp.where(lane // 32 == s, slot_size[q * 4 + s], limit)
        inside = lane % 32 < limit
        for s in range(16):
            both = jnp.logical_and(inside, row < slot_size[s])
            rows = pl.ds(s * 32, 32)
            veff[s, :, q * 128:(q + 1) * 128] = jnp.where(both, green[0, q, rows, :], jnp.zeros((), BF))
            oeff[s, :, q * 128:(q + 1) * 128] = jnp.where(both, green[1, q, rows, :], jnp.zeros((), BF))

    def listed(ref, s):
        return jnp.concatenate([ref[starts[s * 8 + k]] for k in range(8)], axis=0)

    def make_left(dz):
        zz = (z + 4 - dz) % 4
        for dx in range(4):
            arrived(mine.at[zz * 4 + (x + 4 - dx) % 4], mr.at[dz * 4 + dx])
        for xx in range(4):
            s = zz * 4 + xx
            res = jnp.dot(mine[s].reshape(256, 256), listed(veff, s), preferred_element_type=F32)
            left[:, xx * 32:(xx + 1) * 32, :] = res.astype(BF).reshape(8, 32, 512)
        for p in range(8):
            left_t[p, :, pl.ds(pl.multiple_of(zz * 128, 128), 128)] = left[p].T

    loop(0, 4, make_left)

    def make_w(k):
        t = col_to(k)
        lhs = left_t[:, pl.ds(pl.multiple_of(t * 32, 32), 32), :].reshape(256, 512)
        res = lax.dot_general(lhs, listed(oeff, t), NT, preferred_element_type=F32)
        wout[t] = res.astype(BF).reshape(8, 32, 256)

    for k in ORDER:
        make_w(k)
        for dy in (2, 1, 3, 0):
            send_w(dy * 16 + k).start()
    make_w(0)
    for dy in (2, 1, 3):
        send_w(dy * 16).start()
    keep_w = pltpu.make_async_copy(
        wout.at[c, :, pl.ds((y // 2) * 16, 16), pl.ds((y % 2) * 128, 128)], wgot.at[me], wr.at[0])
    keep_w.start()

    def pass_quarter(k):
        quarter(k).wait_recv()
        forward(k).start()

    loop(1, 4, pass_quarter)
    own[3].wait()

    def lay_i(i):
        v = jnp.swapaxes(quart[i // 8, pl.ds(pl.multiple_of(i % 8 * 16, 16), 16)], 0, 1)
        for j in range(16):
            i2[pl.ds(pl.multiple_of(i * 16, 16), 16), j * 128:(j + 1) * 128] = v[j]

    def lay_piece(rr):
        loop(rr * 8, rr * 8 + 8, lay_i)

    loop(0, 4, lambda k: lay_piece(row_to(k)))

    def lay_other(k):
        forward(k).wait_recv()
        lay_piece((y + 4 - k) % 4 * 2 + 1 - core)

    loop(0, 4, lay_other)

    def lay_w(i):
        yy = (y + 4 - i // 8) % 4
        zz = (z + 4 - i // 2 % 4) % 4
        for h in range(2):
            xx = i % 2 * 2 + h
            k = i // 8 * 16 + i // 2 % 4 * 4 + (x + 4 - xx) % 4
            arrived(wgot.at[yy * 16 + zz * 4 + xx], wr.at[k])
        pair = yy * 8 + zz * 2 + i % 2
        v = jnp.swapaxes(wgot[pl.ds(pair * 2, 2)].reshape(16, 16, 128), 0, 1)
        for j in range(16):
            w2[pl.ds(pl.multiple_of(pair * 16, 16), 16), j * 128:(j + 1) * 128] = v[j]

    loop(0, 32, lay_w)

    def multiply(dz):
        zz = (z + dz) % 4
        v = i2[pl.ds(pl.multiple_of(zz * 256, 256), 256), :]
        res = lax.dot_general(v, w2[...], NT, preferred_element_type=F32)
        part[pl.ds(zz * 4, 4)] = res.astype(BF).reshape(4, 64, 512)

    for dz in (2, 1, 3, 0):
        multiply(dz)
        for dx in (2, 1, 3, 0):
            for dy in (2, 1, 3, 0):
                k = dy * 16 + dz * 4 + dx
                if k:
                    send_part(k).start()
    keep_part = pltpu.make_async_copy(
        part.at[c, :, pl.ds(pl.multiple_of(y * 128, 128), 128)], got.at[me], pr.at[0])
    keep_part.start()
    keep_part.wait()
    loop(1, 64, lambda k: send_part(k).wait())
    total = lax.fori_loop(0, 64, lambda i, acc: acc + got[i].astype(F32), jnp.zeros((64, 128), F32), unroll=4)
    out[...] = total.T

    loop(1, 16, lambda k: (green1(k).wait_send(), block(k).wait_send()))
    loop(1, 4, lambda k: (green2(k).wait_send(), quarter(k).wait_send()))
    loop(0, 4, lambda k: (green3(k).wait_send(), forward(k).wait_send()))
    loop(1, 64, lambda k: send_w(k).wait_send())


def shards(integrals, virt_green, occ_green, block_list, block_owner, block_sizes):
    dma = pltpu.SemaphoreType.DMA
    vmem = pltpu.VMEM
    return pl.pallas_call(
        kernel,
        out_shape=jax.ShapeDtypeStruct((128, 64), F32),
        in_specs=[SMEM] * 3 + [ANY] * 3,
        out_specs=VMEM,
        scratch_shapes=[
            pltpu.SMEM((128,), jnp.int32),
            pltpu.SMEM((16,), jnp.int32),
            vmem((2, 32, 512), BF),
            vmem((2, 4, 512, 128), BF),
            vmem((16, 8, 32, 256), BF),
            vmem((8, 128, 16, 128), BF),
            vmem((16, 32, 512), BF),
            vmem((16, 32, 512), BF),
            vmem((8, 128, 512), BF),
            vmem((8, 512, 512), BF),
            vmem((16, 8, 32, 256), BF),
            vmem((64, 8, 16, 128), BF),
            vmem((1024, 2048), BF),
            vmem((512, 2048), BF),
            vmem((16, 64, 512), BF),
            vmem((64, 64, 128), BF),
            dma((16,)), dma((16,)), dma((4,)), dma((4,)), dma((4,)), dma((4,)),
            dma((16,)), dma((16,)), dma((4,)), dma((4,)), dma((4,)), dma((4,)),
            dma((64,)), dma((64,)), dma((64,)), dma((64,)), dma((2,)),
        ],
        compiler_params=pltpu.CompilerParams(
            has_side_effects=True, collective_id=0, vmem_limit_bytes=48 << 20),
    )(block_list, block_owner, block_sizes, integrals, virt_green, occ_green)


def solution(mesh):
    in_specs = (P("row", "col", None), P("col", None), P("col", None), P(), P(), P())
    return jax.shard_map(shards, mesh=mesh, in_specs=in_specs, out_specs=P("row", "col"), check_vma=False)
```

time: 357 us -> 104 us (0.29)
  waiting for transfers between devices: 212 us -> 0 us
  Pallas kernels: 0 us -> 97.5 us
  local copies, waits for them, and re-layouts: 46.8 us -> 5.87 us
  blocking collectives: 38.5 us -> 0 us
  starting transfers between devices: 27 us -> 0 us
  between operations: 15.4 us -> 0.01 us
  matrix products: 12.8 us -> 0 us
    all_to_all x3 -> x0, waiting for transfers between devices: 109 us -> none  [the longest x1 42.1 us: shards(): lax.all_to_all(right_local, 'row', split_axis=2, concat_axis=0, tiled=True)]
    reduce_scatter x2 -> x0, waiting for transfers between devices: 103 us -> none  [the longest x1 72 us: shards(): columns = lax.psum_scatter(total, 'col', scatter_dimension=1, tiled=True)]
    pallas_call x0 -> x1, Pallas kernels: none -> 97.5 us  [shards(): pl.pallas_call(kernel, out_shape=jax.ShapeDtypeStruct((128, 64), F32), in...]
    all_gather x2 -> x0, blocking collectives: 38.5 us -> none  [the longest x1 21 us: shards(): lax.all_gather(virt_green, 'col', axis=0, tiled=True)]
    all_to_all x3 -> x0, starting transfers between devices: 27 us -> none  [the longest x1 16.6 us: shards(): lax.all_to_all(left, 'row', split_axis=2, concat_axis=0, tiled=True)]
    all_to_all x4 -> x0, local copies, waits for them, and re-layouts: 19.9 us -> none  [the longest x2 8.08 us: shards(): lax.all_to_all(right, 'col', split_axis=1, concat_axis=2, tiled=True)]
    dot_general x3 -> x0, matrix products: 12.8 us -> none  [the longest x1 6.1 us: shards(): lax.dot_general(left_share.reshape(left_share.shape[0], -1), right_share....]
    convert_element_type x2 -> x0, local copies, waits for them, and re-layouts: 11.2 us -> none  [the longest x1 6.49 us: shards(): jnp.dot(flat, virt_rows, preferred_element_type=jnp.float32)]
  transfers between devices with their start and end apart: 5 -> 0, of which waited for: 5 -> 0; matrix products, arithmetic and copies ran while one was open for 10% -> 0% of each run, Pallas kernels for 0% -> 0%
where the time goes in v2:
time: 104 us; the launch traced here: 103 us
  Pallas kernels  97.5 us (94%)
  local copies, waits for them, and re-layouts  5.87 us (6%)
    pallas_call x1, Pallas kernels, shards(): pl.pallas_call(kernel, out_shape=jax.ShapeDtypeStruct((128, 64), F32), in...  97.5 us
    unnamed x11, local copies, waits for them, and re-layouts  5.17 us

profile of v2, /device:TPU:1, one launch (start us, length us, event | category | flops | bytes accessed | tf_op | source)
XLA Modules:
  0.0 103.4 jit_solution(17637433146825933502)
XLA Ops:
  0.0 0.8 copy.7.lists
  0.8 0.0 copy-start
  0.8 1.6 %copy-done = bf16[128,32,256]{2,1,0:T(8,128)(2,1)S(1)} copy-done((bf16[128,32,256]{2,1,0:T(8,128)(2,1)S(1)}, bf16[128,32,256]{2,1,0:T(8,128)(2,1)}, u32[]{:S(2)}) %copy-start) | copy-done | bytes 2097176
  2.3 0.0 copy-start.1
  2.4 0.8 copy-done.1
  3.1 0.0 copy-start.2
  3.1 0.8 copy-done.2
  3.9 0.0 copy-start.3
  3.9 0.7 copy-done.3
  4.5 0.0 copy-start.4
  4.5 0.7 copy-done.4
  5.2 97.5 %shard_map.64 = f32[128,64]{1,0:T(8,128)S(1)} custom-call(s32[16,8]{1,0:T(8,128)S(1)} %copy.7.lists, s32[16]{0:T(128)S(1)} %copy-done.3, s32[16]{0:T(128)S(1)} %copy-done.4, bf16[128,32,256]{2,1,0:T(8,128)(2,1)S(1)} %copy-done, bf16[32,512]{1,0:T(8,128)(2,1)S(1)} %copy-done.1, bf16[32,512]{1,0:T(8,128)(2,1)S(1)} %copy-done.2), custom_call_target="tpu_custom_call" | custom-call | tf_op jit(solution)/shard_map/pallas_call | solution.py:257
  102.7 0.7 copy.8
Async XLA Ops:
  0.8 1.6 %copy-start = (bf16[128,32,256]{2,1,0:T(8,128)(2,1)S(1)}, bf16[128,32,256]{2,1,0:T(8,128)(2,1)}, u32[]{:S(2)}) copy-start(bf16[128,32,256]{2,1,0:T(8,128)(2,1)} %ints.1) | copy-start | bytes 6291460
  2.3 0.8 copy-start.1
  3.1 0.8 copy-start.2
  3.9 0.7 copy-start.3
  4.5 0.7 copy-start.4

commit v3 on v2

--- a/solution.py
+++ b/solution.py
@@ -12,7 +12,7 @@
 SMEM = pl.BlockSpec(memory_space=pltpu.SMEM)
 MESH = pl.DeviceIdType.MESH
 NT = (((1,), (1,)), ((), ()))
-ORDER = (10, 15, 4, 9, 14, 3, 8, 13, 2, 7, 12, 1, 6, 11, 5)
+ORDER = (10, 14, 6, 11, 9, 8, 2, 13, 7, 15, 5, 12, 4, 3, 1)
 
 
 def loop(lo, hi, body, unroll=1):
@@ -81,13 +81,11 @@
 
     def send_w(k):
         yy, cc = (y + k // 16) % 4, col_to(k % 16)
-        src = wout.at[cc, :, pl.ds((yy // 2) * 16, 16), pl.ds((yy % 2) * 128, 128)]
-        return remote(src, wgot.at[me], ws.at[k], wr.at[k], yy * 2 + core, cc)
+        return remote(wout.at[cc, yy], wgot.at[me], ws.at[k], wr.at[k], yy * 2 + core, cc)
 
     def send_part(k):
         yy, cc = (y + k // 16) % 4, col_to(k % 16)
-        src = part.at[cc, :, pl.ds(pl.multiple_of(yy * 128, 128), 128)]
-        return remote(src, got.at[me], ps.at[k], pr.at[k], yy * 2 + core, cc)
+        return remote(part.at[cc, yy], got.at[me], ps.at[k], pr.at[k], yy * 2 + core, cc)
 
     own = [
         pltpu.make_async_copy(virt, gsrc.at[0], loc.at[0]),
@@ -115,11 +113,8 @@
     keep.start()
     for k in ORDER:
         green1(k).start()
-    for k in (2, 1, 3):
-        quarter(k).start()
     for k in ORDER:
         block(k).start()
-    send_own().start()
 
     for s in range(16):
         atom = jnp.int32(0)
@@ -127,11 +122,14 @@
             atom = jnp.where(owner[a] == s, a, atom)
         slot_size[s] = sizes[atom]
         for k in range(8):
-            starts[s * 8 + k] = owner[lists[atom, k]]
+            starts[s * 8 + k] = owner[lists[k, atom]]
 
     keep.wait()
     loop(1, 16, lambda k: green1(k).wait_recv())
     loop(1, 4, lambda k: green2(k).start())
+    for k in (2, 1, 3):
+        quarter(k).start()
+    send_own().start()
     green3(0).start()
 
     def pass_green(k):
@@ -174,7 +172,9 @@
         t = col_to(k)
         lhs = left_t[:, pl.ds(pl.multiple_of(t * 32, 32), 32), :].reshape(256, 512)
         res = lax.dot_general(lhs, listed(oeff, t), NT, preferred_element_type=F32)
-        wout[t] = res.astype(BF).reshape(8, 32, 256)
+        res = res.astype(BF).reshape(8, 32, 256)
+        for q in range(4):
+            wout[t, q] = res[:, q // 2 * 16:q // 2 * 16 + 16, q % 2 * 128:q % 2 * 128 + 128]
 
     for k in ORDER:
         make_w(k)
@@ -183,8 +183,7 @@
     make_w(0)
     for dy in (2, 1, 3):
         send_w(dy * 16).start()
-    keep_w = pltpu.make_async_copy(
-        wout.at[c, :, pl.ds((y // 2) * 16, 16), pl.ds((y % 2) * 128, 128)], wgot.at[me], wr.at[0])
+    keep_w = pltpu.make_async_copy(wout.at[c, y], wgot.at[me], wr.at[0])
     keep_w.start()
 
     def pass_quarter(k):
@@ -228,22 +227,25 @@
         zz = (z + dz) % 4
         v = i2[pl.ds(pl.multiple_of(zz * 256, 256), 256), :]
         res = lax.dot_general(v, w2[...], NT, preferred_element_type=F32)
-        part[pl.ds(zz * 4, 4)] = res.astype(BF).reshape(4, 64, 512)
-
-    for dz in (2, 1, 3, 0):
-        multiply(dz)
+        res = res.astype(BF).reshape(4, 64, 512)
+        for q in range(4):
+            part[pl.ds(zz * 4, 4), q] = res[:, :, q * 128:(q + 1) * 128]
+
+    for group in ((2,), (1, 3), (0,)):
+        for dz in group:
+            multiply(dz)
         for dx in (2, 1, 3, 0):
             for dy in (2, 1, 3, 0):
-                k = dy * 16 + dz * 4 + dx
-                if k:
-                    send_part(k).start()
-    keep_part = pltpu.make_async_copy(
-        part.at[c, :, pl.ds(pl.multiple_of(y * 128, 128), 128)], got.at[me], pr.at[0])
+                for dz in group:
+                    k = dy * 16 + dz * 4 + dx
+                    if k:
+                        send_part(k).start()
+    keep_part = pltpu.make_async_copy(part.at[c, y], got.at[me], pr.at[0])
     keep_part.start()
     keep_part.wait()
     loop(1, 64, lambda k: send_part(k).wait())
     total = lax.fori_loop(0, 64, lambda i, acc: acc + got[i].astype(F32), jnp.zeros((64, 128), F32), unroll=4)
-    out[...] = total.T
+    out[...] = total
 
     loop(1, 16, lambda k: (green1(k).wait_send(), block(k).wait_send()))
     loop(1, 4, lambda k: (green2(k).wait_send(), quarter(k).wait_send()))
@@ -254,9 +256,9 @@
 def shards(integrals, virt_green, occ_green, block_list, block_owner, block_sizes):
     dma = pltpu.SemaphoreType.DMA
     vmem = pltpu.VMEM
-    return pl.pallas_call(
+    res = pl.pallas_call(
         kernel,
-        out_shape=jax.ShapeDtypeStruct((128, 64), F32),
+        out_shape=jax.ShapeDtypeStruct((64, 128), F32),
         in_specs=[SMEM] * 3 + [ANY] * 3,
         out_specs=VMEM,
         scratch_shapes=[
@@ -270,19 +272,20 @@
             vmem((16, 32, 512), BF),
             vmem((8, 128, 512), BF),
             vmem((8, 512, 512), BF),
-            vmem((16, 8, 32, 256), BF),
+            vmem((16, 4, 8, 16, 128), BF),
             vmem((64, 8, 16, 128), BF),
             vmem((1024, 2048), BF),
             vmem((512, 2048), BF),
-            vmem((16, 64, 512), BF),
+            vmem((16, 4, 64, 128), BF),
             vmem((64, 64, 128), BF),
             dma((16,)), dma((16,)), dma((4,)), dma((4,)), dma((4,)), dma((4,)),
             dma((16,)), dma((16,)), dma((4,)), dma((4,)), dma((4,)), dma((4,)),
             dma((64,)), dma((64,)), dma((64,)), dma((64,)), dma((2,)),
         ],
         compiler_params=pltpu.CompilerParams(
-            has_side_effects=True, collective_id=0, vmem_limit_bytes=48 << 20),
-    )(block_list, block_owner, block_sizes, integrals, virt_green, occ_green)
+            has_side_effects=True, collective_id=0, vmem_limit_bytes=63 << 20),
+    )(block_list.T, block_owner, block_sizes, integrals, virt_green, occ_green)
+    return res.T
 
 
 def solution(mesh):

time: 104 us -> 91 us (0.88)
  Pallas kernels: 97.5 us -> 89.4 us
  local copies, waits for them, and re-layouts: 5.87 us -> 1.38 us
    pallas_call x1, Pallas kernels: 97.5 us -> 89.4 us  [shards(): pl.pallas_call(kernel, out_shape=jax.ShapeDtypeStruct((64, 128), F32), in...]
    unnamed x11 -> x1, local copies, waits for them, and re-layouts: 5.17 us -> 1.38 us
where the time goes in v3:
time: 91 us; the launch traced here: 90.8 us
  Pallas kernels  89.4 us (98%)
  local copies, waits for them, and re-layouts  1.38 us (2%)
    pallas_call x1, Pallas kernels, shards(): pl.pallas_call(kernel, out_shape=jax.ShapeDtypeStruct((64, 128), F32), in...  89.4 us

profile of v3, /device:TPU:1, one launch (start us, length us, event | category | flops | bytes accessed | tf_op | source)
XLA Modules:
  0.0 90.8 jit_solution(2219388218768411885)
XLA Ops:
  0.0 89.4 %shard_map.64 = f32[64,128]{1,0:T(8,128)} custom-call(s32[8,16]{1,0:T(8,128)} %bitcast.3, s32[16]{0:T(128)} %owner.1, s32[16]{0:T(128)} %sizes.1, bf16[128,32,256]{2,1,0:T(8,128)(2,1)} %ints.1, bf16[32,512]{1,0:T(8,128)(2,1)} %virt.1, bf16[32,512]{1,0:T(8,128)(2,1)} %occ.1), custom_call_target="tpu_custom_call" | custom-call | tf_op jit(solution)/shard_map/pallas_call | solution.py:259
  89.4 1.4 %copy.8 = f32[128,64]{0,1:T(8,128)} copy(f32[128,64]{0,1:T(8,128)} %bitcast.2) | data formatting | bytes 65536

commit v4 on v0

v4 whole, which is shorter than its diff:
```python
import jax
import jax.numpy as jnp
from jax import lax
from jax.experimental import pallas as pl
from jax.experimental.pallas import tpu as pltpu
from jax.sharding import PartitionSpec as P

BF = jnp.bfloat16
F32 = jnp.float32
ANY = pl.BlockSpec(memory_space=pl.ANY)
VMEM = pl.BlockSpec(memory_space=pltpu.VMEM)
SMEM = pl.BlockSpec(memory_space=pltpu.SMEM)
MESH = pl.DeviceIdType.MESH
NT = (((1,), (1,)), ((), ()))
ORDER = (10, 14, 6, 11, 9, 8, 2, 13, 7, 15, 5, 12, 4, 3, 1)


def loop(lo, hi, body, unroll=1):
    def step(i, carry):
        body(i)
        return carry

    lax.fori_loop(lo, hi, step, 0, unroll=unroll)


def remote(src, dst, ssem, rsem, row, col):
    return pltpu.make_async_remote_copy(
        src_ref=src, dst_ref=dst, send_sem=ssem, recv_sem=rsem, device_id=(row, col), device_id_type=MESH,
    )


def arrived(ref, sem):
    pltpu.make_async_copy(ref, ref, sem).wait()


def kernel(lists_in, owner_in, sizes_in, ints, virt, occ, out,
           lists, owner, sizes, starts, slot_size, vall, oall, mine, quart, veff, oeff, left, left_t, wout, wgot, i2, w2, half0, part, got,
           loc, v1s, v1r, v2s, v2r, o1s, o1r, o2s, o2r, ms, mr, qs, qr, fs, fr, ws, wr, ps, pr):
    r = lax.axis_index("row")
    c = lax.axis_index("col")
    y, core = r >> 1, r & 1
    z, x = c >> 2, c & 3
    me = y * 16 + c
    twin = y * 2 + (1 - core)

    cols = [((z + k // 4) & 3) * 4 + ((x + k % 4) & 3) for k in range(16)]
    ys = [(y + k) & 3 for k in range(4)]

    def col_to(k):
        return cols[k] if isinstance(k, int) else ((z + (k >> 2)) & 3) * 4 + ((x + (k & 3)) & 3)

    def y_to(k):
        return ys[k] if isinstance(k, int) else (y + k) & 3

    def row_to(k):
        return y_to(k) * 2 + core

    def piece(yy, u):
        return ints.at[pl.ds(u * 64, 64), pl.ds((yy >> 1) * 16, 16), pl.ds((yy & 1) * 128, 128)]

    half_rows = pl.ds(core * 16, 16)

    def virt1(k):
        return remote(virt.at[half_rows], vall.at[c, half_rows], v1s.at[k], v1r.at[k], r, col_to(k))

    def virt2():
        part = vall.at[:, half_rows]
        return remote(part, part, v2s.at[0], v2r.at[0], twin, c)

    def occ1(k):
        return remote(occ.at[half_rows], oall.at[c, half_rows], o1s.at[k], o1r.at[k], r, col_to(k))

    def occ2():
        part = oall.at[:, half_rows]
        return remote(part, part, o2s.at[0], o2r.at[0], twin, c)

    def block(h, k):
        src = ints.at[pl.ds(h * 64 + col_to(k) * 4, 4)]
        return remote(src, mine.at[h, c], ms.at[h * 16 + k], mr.at[h * 16 + k], r, col_to(k))

    def quarter(u, k):
        dst = quart.at[r, pl.ds(u * 64, 64)]
        return remote(piece(y_to(k), u), dst, qs.at[u * 4 + k], qr.at[u * 4 + k], row_to(k), c)

    def forward(u, k):
        part = quart.at[((y - k) & 3) * 2 + core, pl.ds(u * 64, 64)]
        return remote(part, part, fs.at[u * 4 + k], fr.at[u * 4 + k], twin, c)

    def send_own(u):
        dst = quart.at[r, pl.ds(u * 64, 64)]
        return remote(piece(y, u), dst, fs.at[u * 4], fr.at[u * 4], twin, c)

    def send_w(h, k):
        yy, cc = y_to(k >> 4), col_to(k & 15)
        at = h * 64 + k
        return remote(wout.at[h, cc, yy], wgot.at[h, me], ws.at[at], wr.at[at], yy * 2 + core, cc)

    def send_part(k):
        yy, cc = y_to(k >> 4), col_to(k & 15)
        return remote(part.at[cc, yy], got.at[me], ps.at[0], pr.at[0], yy * 2 + core, cc)

    tables = [
        pltpu.make_async_copy(src, dst, loc.at[i])
        for i, (src, dst) in enumerate(((lists_in, lists), (owner_in, owner), (sizes_in, sizes)))
    ]
    own = [
        pltpu.make_async_copy(virt.at[half_rows], vall.at[c, half_rows], v1r.at[0]),
        pltpu.make_async_copy(occ.at[half_rows], oall.at[c, half_rows], o1r.at[0]),
        pltpu.make_async_copy(ints.at[pl.ds(c * 4, 4)], mine.at[0, c], mr.at[0]),
        pltpu.make_async_copy(ints.at[pl.ds(64 + c * 4, 4)], mine.at[1, c], mr.at[16]),
        pltpu.make_async_copy(piece(y, 0), quart.at[r, pl.ds(0, 64)], qr.at[0]),
        pltpu.make_async_copy(piece(y, 1), quart.at[r, pl.ds(64, 64)], qr.at[4]),
    ]
    for copy in tables + own:
        copy.start()

    barrier = pltpu.get_barrier_semaphore()

    def greet(row, col):
        pl.semaphore_signal(barrier, inc=1, device_id=(row, col), device_id_type=MESH)

    loop(1, 16, lambda k: greet(r, col_to(k)))
    loop(1, 4, lambda k: greet(row_to(k), c))
    greet(twin, c)

    pl.semaphore_wait(barrier, 19)
    for k in (2, 1, 3):
        quarter(0, k).start()
    for k in ORDER:
        virt1(k).start()
    for k in ORDER:
        occ1(k).start()
    for k in ORDER:
        block(0, k).start()
    send_own(0).start()

    for copy in tables:
        copy.wait()
    for s in range(16):
        atom = jnp.int32(0)
        for a in range(16):
            atom = jnp.where(owner[a] == s, a, atom)
        slot_size[s] = sizes[atom]
        for k in range(8):
            starts[s * 8 + k] = owner[lists[k, atom]]

    own[0].wait()
    loop(1, 16, lambda k: virt1(k).wait_recv())
    virt2().start()
    own[1].wait()
    loop(1, 16, lambda k: occ1(k).wait_recv())
    occ2().start()
    for i, k in enumerate(ORDER):
        block(1, k).start()
        if i % 5 == 1:
            quarter(1, (2, 1, 3)[i // 5]).start()
    send_own(1).start()
    virt2().wait_recv()

    lane = lax.broadcasted_iota(jnp.int32, (32, 512), 1)
    row = lax.broadcasted_iota(jnp.int32, (32, 512), 0)
    limit = jnp.zeros((32, 512), jnp.int32)
    for s in range(16):
        limit = jnp.where(lane // 32 == s, slot_size[s], limit)
    inside = lane % 32 < limit

    def mask(ref, dst):
        def one(s):
            both = jnp.logical_and(inside, row < slot_size[s])
            dst[s] = jnp.where(both, ref[s], jnp.zeros((), BF))

        loop(0, 16, one, 4)

    mask(vall, veff)

    def listed(ref, s):
        return jnp.concatenate([ref[starts[s * 8 + k]] for k in range(8)], axis=0)

    def make_left(h, i):
        dz = (2 + i) & 3
        zz = ((z - dz) & 3)
        for dx in range(4):
            arrived(mine.at[h, zz * 4 + ((x - dx) & 3)], mr.at[h * 16 + dz * 4 + dx])
        for xx in range(4):
            s = zz * 4 + xx
            res = jnp.dot(mine[h, s].reshape(128, 256), listed(veff, s), preferred_element_type=F32)
            left[:, xx * 32:(xx + 1) * 32, :] = res.astype(BF).reshape(4, 32, 512)
        for p in range(4):
            left_t[p, :, pl.ds(pl.multiple_of(zz * 128, 128), 128)] = left[p].T

    def make_w(h, k):
        t = col_to(k)
        lhs = left_t[:, pl.ds(pl.multiple_of(t * 32, 32), 32), :].reshape(128, 512)
        res = lax.dot_general(lhs, listed(oeff, t), NT, preferred_element_type=F32)
        res = res.astype(BF).reshape(4, 32, 256)
        for q in range(4):
            wout[h, t, q] = res[:, q // 2 * 16:q // 2 * 16 + 16, q % 2 * 128:q % 2 * 128 + 128]

    def pass_quarter(u):
        def one(k):
            quarter(u, k).wait_recv()
            forward(u, k).start()

        loop(1, 4, one)
        own[4 + u].wait()

    def lay_i(i):
        v = jnp.swapaxes(quart[i // 8, pl.ds(pl.multiple_of(i % 8 * 16, 16), 16)], 0, 1)
        for j in range(16):
            i2[pl.ds(pl.multiple_of(i * 16, 16), 16), j * 128:(j + 1) * 128] = v[j]

    def lay_piece(u, rr):
        loop(rr * 8 + u * 4, rr * 8 + u * 4 + 4, lay_i)

    def half(h):
        @pl.when(h == 1)
        def _():
            pass_quarter(0)
            loop(0, 4, lambda k: lay_piece(0, row_to(k)))

        loop(0, 4, lambda i: make_left(h, i))

        @pl.when(h == 0)
        def _():
            occ2().wait_recv()
            mask(oall, oeff)

        for k in ORDER:
            make_w(h, k)
            for dy in (2, 1, 3, 0):
                send_w(h, dy * 16 + k).start()
        make_w(h, 0)
        for dy in (2, 1, 3):
            send_w(h, dy * 16).start()
        pltpu.make_async_copy(wout.at[h, c, y], wgot.at[h, me], wr.at[h * 64]).start()

    loop(0, 2, half)

    pass_quarter(1)

    def lay_other(u, k):
        forward(u, k).wait_recv()
        lay_piece(u, ((y - k) & 3) * 2 + 1 - core)

    loop(0, 4, lambda k: lay_other(0, k))
    loop(0, 4, lambda k: lay_piece(1, row_to(k)))
    loop(0, 4, lambda k: lay_other(1, k))

    def lay_w(h, i):
        dy, dz = i // 4, i % 4
        yy = ((y - dy) & 3)
        first = yy * 16 + ((z - dz) & 3) * 4
        for dx in range(4):
            arrived(wgot.at[h, first + ((x - dx) & 3)], wr.at[h * 64 + dy * 16 + dz * 4 + dx])
        v = jnp.swapaxes(wgot[h, pl.ds(first, 4)].reshape(16, 16, 128), 0, 1)
        at = (yy + h * (1 - 2 * (yy % 2))) * 64 + first % 16 * 4
        for j in range(16):
            w2[h, pl.ds(pl.multiple_of(at, 16), 16), j * 128:(j + 1) * 128] = v[j]

    def product(h, at, size):
        v = i2[pl.ds(pl.multiple_of(at, size), size), :]
        return lax.dot_general(v, w2[h], NT, preferred_element_type=F32).astype(BF)

    def multiply0(i):
        half0[pl.ds(pl.multiple_of(i * 512, 512), 512), :] = product(0, i * 512, 512)

    low = lax.broadcasted_iota(jnp.int32, (256, 128), 1) < 64

    def multiply1(dz):
        zz = (z + dz) & 3
        res = product(1, zz * 256, 256)
        old = half0[pl.ds(pl.multiple_of(zz * 256, 256), 256), :]
        for q in range(2):
            one, two = old[:, q * 128:(q + 1) * 128], res[:, q * 128:(q + 1) * 128]
            part[pl.ds(zz * 4, 4), q * 2] = jnp.where(low, one, two).reshape(4, 64, 128)
            part[pl.ds(zz * 4, 4), q * 2 + 1] = jnp.where(low, two, one).reshape(4, 64, 128)

    loop(0, 16, lambda i: lay_w(0, i))
    loop(0, 2, multiply0)
    loop(0, 16, lambda i: lay_w(1, i))
    for group in ((2,), (1, 3), (0,)):
        for dz in group:
            multiply1(dz)
        for dx in (2, 1, 3, 0):
            for dy in (2, 1, 3, 0):
                for dz in group:
                    k = dy * 16 + dz * 4 + dx
                    if k:
                        send_part(k).start()
    pltpu.make_async_copy(part.at[c, y], got.at[me], pr.at[0]).start()

    loop(1, 16, lambda k: (virt1(k).wait_send(), occ1(k).wait_send()))
    loop(1, 16, lambda k: (block(0, k).wait_send(), block(1, k).wait_send()))
    loop(1, 4, lambda k: (quarter(0, k).wait_send(), quarter(1, k).wait_send()))
    virt2().wait_send()
    occ2().wait_send()
    loop(0, 4, lambda k: (forward(0, k).wait_send(), forward(1, k).wait_send()))
    loop(1, 64, lambda k: (send_w(0, k).wait_send(), send_w(1, k).wait_send()))
    arrived(got, pr.at[0])
    total = lax.fori_loop(0, 64, lambda i, acc: acc + got[i].astype(F32), jnp.zeros((64, 128), F32), unroll=4)
    out[...] = jnp.where((y & 1) == 1, pltpu.roll(total, 64, 1), total)

    arrived(got.at[pl.ds(0, 63)], ps.at[0])


def shards(integrals, virt_green, occ_green, block_list, block_owner, block_sizes):
    dma = pltpu.SemaphoreType.DMA
    vmem = pltpu.VMEM
    res = pl.pallas_call(
        kernel,
        out_shape=jax.ShapeDtypeStruct((64, 128), F32),
        in_specs=[ANY] * 6,
        out_specs=VMEM,
        scratch_shapes=[
            pltpu.SMEM((8, 16), jnp.int32),
            pltpu.SMEM((16,), jnp.int32),
            pltpu.SMEM((16,), jnp.int32),
            pltpu.SMEM((128,), jnp.int32),
            pltpu.SMEM((16,), jnp.int32),
            vmem((16, 32, 512), BF),
            vmem((16, 32, 512), BF),
            vmem((2, 16, 4, 32, 256), BF),
            vmem((8, 128, 16, 128), BF),
            vmem((16, 32, 512), BF),
            vmem((16, 32, 512), BF),
            vmem((4, 128, 512), BF),
            vmem((4, 512, 512), BF),
            vmem((2, 16, 4, 4, 16, 128), BF),
            vmem((2, 64, 4, 16, 128), BF),
            vmem((1024, 2048), BF),
            vmem((2, 256, 2048), BF),
            vmem((1024, 256), BF),
            vmem((16, 4, 64, 128), BF),
            vmem((64, 64, 128), BF),
            dma((3,)), dma((16,)), dma((16,)), dma((1,)), dma((1,)),
            dma((16,)), dma((16,)), dma((1,)), dma((1,)),
            dma((32,)), dma((32,)), dma((8,)), dma((8,)), dma((8,)), dma((8,)),
            dma((128,)), dma((128,)), dma((1,)), dma((1,)),
        ],
        compiler_params=pltpu.CompilerParams(
            has_side_effects=True, collective_id=0, vmem_limit_bytes=63 << 20),
    )(block_list.T, block_owner, block_sizes, integrals, virt_green, occ_green)
    return res.T


def solution(mesh):
    in_specs = (P("row", "col", None), P("col", None), P("col", None), P(), P(), P())
    return jax.shard_map(shards, mesh=mesh, in_specs=in_specs, out_specs=P("row", "col"), check_vma=False)
```

time: 357 us -> 86.2 us (0.24)
  waiting for transfers between devices: 212 us -> 0 us
  Pallas kernels: 0 us -> 83.8 us
  local copies, waits for them, and re-layouts: 46.8 us -> 1.38 us
  blocking collectives: 38.5 us -> 0 us
  starting transfers between devices: 27 us -> 0 us
  between operations: 15.4 us -> 0.01 us
  matrix products: 12.8 us -> 0 us
    all_to_all x3 -> x0, waiting for transfers between devices: 109 us -> none  [the longest x1 42.1 us: shards(): lax.all_to_all(right_local, 'row', split_axis=2, concat_axis=0, tiled=True)]
    reduce_scatter x2 -> x0, waiting for transfers between devices: 103 us -> none  [the longest x1 72 us: shards(): columns = lax.psum_scatter(total, 'col', scatter_dimension=1, tiled=True)]
    pallas_call x0 -> x1, Pallas kernels: none -> 83.8 us  [shards(): pl.pallas_call(kernel, out_shape=jax.ShapeDtypeStruct((64, 128), F32), in...]
    all_gather x2 -> x0, blocking collectives: 38.5 us -> none  [the longest x1 21 us: shards(): lax.all_gather(virt_green, 'col', axis=0, tiled=True)]
    all_to_all x3 -> x0, starting transfers between devices: 27 us -> none  [the longest x1 16.6 us: shards(): lax.all_to_all(left, 'row', split_axis=2, concat_axis=0, tiled=True)]
    all_to_all x4 -> x0, local copies, waits for them, and re-layouts: 19.9 us -> none  [the longest x2 8.08 us: shards(): lax.all_to_all(right, 'col', split_axis=1, concat_axis=2, tiled=True)]
    dot_general x3 -> x0, matrix products: 12.8 us -> none  [the longest x1 6.1 us: shards(): lax.dot_general(left_share.reshape(left_share.shape[0], -1), right_share....]
    convert_element_type x2 -> x0, local copies, waits for them, and re-layouts: 11.2 us -> none  [the longest x1 6.49 us: shards(): jnp.dot(flat, virt_rows, preferred_element_type=jnp.float32)]
  transfers between devices with their start and end apart: 5 -> 0, of which waited for: 5 -> 0; matrix products, arithmetic and copies ran while one was open for 10% -> 0% of each run, Pallas kernels for 0% -> 0%
where the time goes in v4:
time: 86.2 us; the launch traced here: 85.2 us
  Pallas kernels  83.8 us (97%)
  local copies, waits for them, and re-layouts  1.38 us (2%)
    pallas_call x1, Pallas kernels, shards(): pl.pallas_call(kernel, out_shape=jax.ShapeDtypeStruct((64, 128), F32), in...  83.8 us

profile of v4, /device:TPU:1, one launch (start us, length us, event | category | flops | bytes accessed | tf_op | source)
XLA Modules:
  0.0 85.2 jit_solution(18179347575392273486)
XLA Ops:
  0.0 83.8 %shard_map.64 = f32[64,128]{1,0:T(8,128)} custom-call(s32[8,16]{1,0:T(8,128)} %bitcast.3, s32[16]{0:T(128)} %owner_in.1, s32[16]{0:T(128)} %sizes_in.1, bf16[128,32,256]{2,1,0:T(8,128)(2,1)} %ints.1, bf16[32,512]{1,0:T(8,128)(2,1)} %virt.1, bf16[32,512]{1,0:T(8,128)(2,1)} %occ.1), custom_call_target="tpu_custom_call" | custom-call | tf_op jit(solution)/shard_map/pallas_call | solution.py:309
  83.8 1.4 %copy.8 = f32[128,64]{0,1:T(8,128)} copy(f32[128,64]{0,1:T(8,128)} %bitcast.2) | data formatting | bytes 65536

commit v5 on v4

--- a/solution.py
+++ b/solution.py
@@ -13,6 +13,7 @@
 MESH = pl.DeviceIdType.MESH
 NT = (((1,), (1,)), ((), ()))
 ORDER = (10, 14, 6, 11, 9, 8, 2, 13, 7, 15, 5, 12, 4, 3, 1)
+MIXED = (10, 1, 14, 4, 6, 3, 11, 12, 9, 2, 8, 5, 7, 13, 15, 0)
 
 
 def loop(lo, hi, body, unroll=1):
@@ -150,11 +151,16 @@
     own[1].wait()
     loop(1, 16, lambda k: occ1(k).wait_recv())
     occ2().start()
-    for i, k in enumerate(ORDER):
+    for k in (2, 1, 3):
+        quarter(1, k).start()
+    send_own(1).start()
+
+    def second(k):
+        block(0, k).wait_send()
         block(1, k).start()
-        if i % 5 == 1:
-            quarter(1, (2, 1, 3)[i // 5]).start()
-    send_own(1).start()
+
+    for k in ORDER[:8]:
+        second(k)
     virt2().wait_recv()
 
     lane = lax.broadcasted_iota(jnp.int32, (32, 512), 1)
@@ -172,6 +178,8 @@
         loop(0, 16, one, 4)
 
     mask(vall, veff)
+    for k in ORDER[8:]:
+        second(k)
 
     def listed(ref, s):
         return jnp.concatenate([ref[starts[s * 8 + k]] for k in range(8)], axis=0)
@@ -213,11 +221,6 @@
         loop(rr * 8 + u * 4, rr * 8 + u * 4 + 4, lay_i)
 
     def half(h):
-        @pl.when(h == 1)
-        def _():
-            pass_quarter(0)
-            loop(0, 4, lambda k: lay_piece(0, row_to(k)))
-
         loop(0, 4, lambda i: make_left(h, i))
 
         @pl.when(h == 0)
@@ -225,25 +228,27 @@
             occ2().wait_recv()
             mask(oall, oeff)
 
-        for k in ORDER:
-            make_w(h, k)
-            for dy in (2, 1, 3, 0):
-                send_w(h, dy * 16 + k).start()
-        make_w(h, 0)
-        for dy in (2, 1, 3):
-            send_w(h, dy * 16).start()
+        for g in range(0, 16, 4):
+            for k in MIXED[g:g + 4]:
+                make_w(h, k)
+            for k in MIXED[g:g + 4]:
+                for dy in (2, 1, 3, 0):
+                    if dy * 16 + k:
+                        send_w(h, dy * 16 + k).start()
         pltpu.make_async_copy(wout.at[h, c, y], wgot.at[h, me], wr.at[h * 64]).start()
 
     loop(0, 2, half)
 
+    pass_quarter(0)
     pass_quarter(1)
 
     def lay_other(u, k):
         forward(u, k).wait_recv()
         lay_piece(u, ((y - k) & 3) * 2 + 1 - core)
 
+    loop(0, 4, lambda k: lay_piece(0, row_to(k)))
+    loop(0, 4, lambda k: lay_piece(1, row_to(k)))
     loop(0, 4, lambda k: lay_other(0, k))
-    loop(0, 4, lambda k: lay_piece(1, row_to(k)))
     loop(0, 4, lambda k: lay_other(1, k))
 
     def lay_w(h, i):
@@ -290,7 +295,7 @@
     pltpu.make_async_copy(part.at[c, y], got.at[me], pr.at[0]).start()
 
     loop(1, 16, lambda k: (virt1(k).wait_send(), occ1(k).wait_send()))
-    loop(1, 16, lambda k: (block(0, k).wait_send(), block(1, k).wait_send()))
+    loop(1, 16, lambda k: block(1, k).wait_send())
     loop(1, 4, lambda k: (quarter(0, k).wait_send(), quarter(1, k).wait_send()))
     virt2().wait_send()
     occ2().wait_send()

time: 86.2 us -> 82.8 us (0.961)
  Pallas kernels: 83.8 us -> 81.1 us
    pallas_call x1, Pallas kernels: 83.8 us -> 81.1 us  [shards(): pl.pallas_call(kernel, out_shape=jax.ShapeDtypeStruct((64, 128), F32), in...]
where the time goes in v5:
time: 82.8 us; the launch traced here: 82.5 us
  Pallas kernels  81.1 us (98%)
  local copies, waits for them, and re-layouts  1.38 us (2%)
    pallas_call x1, Pallas kernels, shards(): pl.pallas_call(kernel, out_shape=jax.ShapeDtypeStruct((64, 128), F32), in...  81.1 us

profile of v5, /device:TPU:1, one launch (start us, length us, event | category | flops | bytes accessed | tf_op | source)
XLA Modules:
  0.0 82.5 jit_solution(2842517265673767931)
XLA Ops:
  0.0 81.1 %shard_map.64 = f32[64,128]{1,0:T(8,128)} custom-call(s32[8,16]{1,0:T(8,128)} %bitcast.3, s32[16]{0:T(128)} %owner_in.1, s32[16]{0:T(128)} %sizes_in.1, bf16[128,32,256]{2,1,0:T(8,128)(2,1)} %ints.1, bf16[32,512]{1,0:T(8,128)(2,1)} %virt.1, bf16[32,512]{1,0:T(8,128)(2,1)} %occ.1), custom_call_target="tpu_custom_call" | custom-call | tf_op jit(solution)/shard_map/pallas_call | solution.py:314
  81.1 1.4 %copy.8 = f32[128,64]{0,1:T(8,128)} copy(f32[128,64]{0,1:T(8,128)} %bitcast.2) | data formatting | bytes 65536

commit v6 on v5

--- a/solution.py
+++ b/solution.py
@@ -36,7 +36,7 @@
 
 def kernel(lists_in, owner_in, sizes_in, ints, virt, occ, out,
            lists, owner, sizes, starts, slot_size, vall, oall, mine, quart, veff, oeff, left, left_t, wout, wgot, i2, w2, half0, part, got,
-           loc, v1s, v1r, v2s, v2r, o1s, o1r, o2s, o2r, ms, mr, qs, qr, fs, fr, ws, wr, ps, pr):
+           loc, v1s, v1r, v2s, v2r, o1s, o1r, o2s, o2r, o3s, o3r, ms, mr, qs, qr, fs, fr, ws, wr, ps, pr):
     r = lax.axis_index("row")
     c = lax.axis_index("col")
     y, core = r >> 1, r & 1
@@ -68,12 +68,18 @@
         part = vall.at[:, half_rows]
         return remote(part, part, v2s.at[0], v2r.at[0], twin, c)
 
+    occ_piece = occ.at[half_rows, pl.ds(pl.multiple_of(y * 128, 128), 128)]
+
     def occ1(k):
-        return remote(occ.at[half_rows], oall.at[c, half_rows], o1s.at[k], o1r.at[k], r, col_to(k))
-
-    def occ2():
-        part = oall.at[:, half_rows]
-        return remote(part, part, o2s.at[0], o2r.at[0], twin, c)
+        return remote(occ_piece, oall.at[y, c, half_rows], o1s.at[k], o1r.at[k], r, col_to(k))
+
+    def occ2(k):
+        part = oall.at[y, :, half_rows]
+        return remote(part, part, o2s.at[k], o2r.at[k], row_to(k), c)
+
+    def occ3(k):
+        part = oall.at[(y - k) & 3, :, half_rows]
+        return remote(part, part, o3s.at[k], o3r.at[k], twin, c)
 
     def block(h, k):
         src = ints.at[pl.ds(h * 64 + col_to(k) * 4, 4)]
@@ -106,7 +112,7 @@
     ]
     own = [
         pltpu.make_async_copy(virt.at[half_rows], vall.at[c, half_rows], v1r.at[0]),
-        pltpu.make_async_copy(occ.at[half_rows], oall.at[c, half_rows], o1r.at[0]),
+        pltpu.make_async_copy(occ_piece, oall.at[y, c, half_rows], o1r.at[0]),
         pltpu.make_async_copy(ints.at[pl.ds(c * 4, 4)], mine.at[0, c], mr.at[0]),
         pltpu.make_async_copy(ints.at[pl.ds(64 + c * 4, 4)], mine.at[1, c], mr.at[16]),
         pltpu.make_async_copy(piece(y, 0), quart.at[r, pl.ds(0, 64)], qr.at[0]),
@@ -150,7 +156,8 @@
     virt2().start()
     own[1].wait()
     loop(1, 16, lambda k: occ1(k).wait_recv())
-    occ2().start()
+    loop(1, 4, lambda k: occ2(k).start())
+    occ3(0).start()
     for k in (2, 1, 3):
         quarter(1, k).start()
     send_own(1).start()
@@ -170,14 +177,19 @@
         limit = jnp.where(lane // 32 == s, slot_size[s], limit)
     inside = lane % 32 < limit
 
-    def mask(ref, dst):
+    def mask(load, dst):
         def one(s):
             both = jnp.logical_and(inside, row < slot_size[s])
-            dst[s] = jnp.where(both, ref[s], jnp.zeros((), BF))
+            dst[s] = jnp.where(both, load(s), jnp.zeros((), BF))
 
         loop(0, 16, one, 4)
 
-    mask(vall, veff)
+    mask(lambda s: vall[s], veff)
+    def pass_occ(k):
+        occ2(k).wait_recv()
+        occ3(k).start()
+
+    loop(1, 4, pass_occ)
     for k in ORDER[8:]:
         second(k)
 
@@ -225,8 +237,8 @@
 
         @pl.when(h == 0)
         def _():
-            occ2().wait_recv()
-            mask(oall, oeff)
+            loop(0, 4, lambda k: occ3(k).wait_recv())
+            mask(lambda s: jnp.concatenate([oall[q, s] for q in range(4)], axis=1), oeff)
 
         for g in range(0, 16, 4):
             for k in MIXED[g:g + 4]:
@@ -298,7 +310,8 @@
     loop(1, 16, lambda k: block(1, k).wait_send())
     loop(1, 4, lambda k: (quarter(0, k).wait_send(), quarter(1, k).wait_send()))
     virt2().wait_send()
-    occ2().wait_send()
+    loop(1, 4, lambda k: occ2(k).wait_send())
+    loop(0, 4, lambda k: occ3(k).wait_send())
     loop(0, 4, lambda k: (forward(0, k).wait_send(), forward(1, k).wait_send()))
     loop(1, 64, lambda k: (send_w(0, k).wait_send(), send_w(1, k).wait_send()))
     arrived(got, pr.at[0])
@@ -323,7 +336,7 @@
             pltpu.SMEM((128,), jnp.int32),
             pltpu.SMEM((16,), jnp.int32),
             vmem((16, 32, 512), BF),
-            vmem((16, 32, 512), BF),
+            vmem((4, 16, 32, 128), BF),
             vmem((2, 16, 4, 32, 256), BF),
             vmem((8, 128, 16, 128), BF),
             vmem((16, 32, 512), BF),
@@ -338,7 +351,7 @@
             vmem((16, 4, 64, 128), BF),
             vmem((64, 64, 128), BF),
             dma((3,)), dma((16,)), dma((16,)), dma((1,)), dma((1,)),
-            dma((16,)), dma((16,)), dma((1,)), dma((1,)),
+            dma((16,)), dma((16,)), dma((4,)), dma((4,)), dma((4,)), dma((4,)),
             dma((32,)), dma((32,)), dma((8,)), dma((8,)), dma((8,)), dma((8,)),
             dma((128,)), dma((128,)), dma((1,)), dma((1,)),
         ],

time: 82.8 us -> 81 us (0.978)
  Pallas kernels: 81.1 us -> 79.5 us
    pallas_call x1, Pallas kernels: 81.1 us -> 79.5 us  [shards(): pl.pallas_call(kernel, out_shape=jax.ShapeDtypeStruct((64, 128), F32), in...]
where the time goes in v6:
time: 81 us; the launch traced here: 80.8 us
  Pallas kernels  79.5 us (98%)
  local copies, waits for them, and re-layouts  1.38 us (2%)
    pallas_call x1, Pallas kernels, shards(): pl.pallas_call(kernel, out_shape=jax.ShapeDtypeStruct((64, 128), F32), in...  79.5 us

profile of v6, /device:TPU:1, one launch (start us, length us, event | category | flops | bytes accessed | tf_op | source)
XLA Modules:
  0.0 80.8 jit_solution(10722746823446546815)
XLA Ops:
  0.0 79.5 %shard_map.64 = f32[64,128]{1,0:T(8,128)} custom-call(s32[8,16]{1,0:T(8,128)} %bitcast.3, s32[16]{0:T(128)} %owner_in.1, s32[16]{0:T(128)} %sizes_in.1, bf16[128,32,256]{2,1,0:T(8,128)(2,1)} %ints.1, bf16[32,512]{1,0:T(8,128)(2,1)} %virt.1, bf16[32,512]{1,0:T(8,128)(2,1)} %occ.1), custom_call_target="tpu_custom_call" | custom-call | tf_op jit(solution)/shard_map/pallas_call | solution.py:327
  79.5 1.4 %copy.8 = f32[128,64]{0,1:T(8,128)} copy(f32[128,64]{0,1:T(8,128)} %bitcast.2) | data formatting | bytes 65536

commit v7 on v6

--- a/solution.py
+++ b/solution.py
@@ -104,7 +104,7 @@
 
     def send_part(k):
         yy, cc = y_to(k >> 4), col_to(k & 15)
-        return remote(part.at[cc, yy], got.at[me], ps.at[0], pr.at[0], yy * 2 + core, cc)
+        return remote(part.at[cc, yy], got.at[z * 16 + y * 4 + x], ps.at[0], pr.at[(k >> 2) & 3], yy * 2 + core, cc)
 
     tables = [
         pltpu.make_async_copy(src, dst, loc.at[i])
@@ -304,7 +304,7 @@
                     k = dy * 16 + dz * 4 + dx
                     if k:
                         send_part(k).start()
-    pltpu.make_async_copy(part.at[c, y], got.at[me], pr.at[0]).start()
+    pltpu.make_async_copy(part.at[c, y], got.at[z * 16 + y * 4 + x], pr.at[0]).start()
 
     loop(1, 16, lambda k: (virt1(k).wait_send(), occ1(k).wait_send()))
     loop(1, 16, lambda k: block(1, k).wait_send())
@@ -314,8 +314,11 @@
     loop(0, 4, lambda k: occ3(k).wait_send())
     loop(0, 4, lambda k: (forward(0, k).wait_send(), forward(1, k).wait_send()))
     loop(1, 64, lambda k: (send_w(0, k).wait_send(), send_w(1, k).wait_send()))
-    arrived(got, pr.at[0])
-    total = lax.fori_loop(0, 64, lambda i, acc: acc + got[i].astype(F32), jnp.zeros((64, 128), F32), unroll=4)
+    total = jnp.zeros((64, 128), F32)
+    for dz in (2, 1, 3, 0):
+        first = ((z - dz) & 3) * 16
+        arrived(got.at[pl.ds(first, 16)], pr.at[dz])
+        total = lax.fori_loop(0, 16, lambda i, acc, at=first: acc + got[at + i].astype(F32), total, unroll=16)
     out[...] = jnp.where((y & 1) == 1, pltpu.roll(total, 64, 1), total)
 
     arrived(got.at[pl.ds(0, 63)], ps.at[0])
@@ -353,7 +356,7 @@
             dma((3,)), dma((16,)), dma((16,)), dma((1,)), dma((1,)),
             dma((16,)), dma((16,)), dma((4,)), dma((4,)), dma((4,)), dma((4,)),
             dma((32,)), dma((32,)), dma((8,)), dma((8,)), dma((8,)), dma((8,)),
-            dma((128,)), dma((128,)), dma((1,)), dma((1,)),
+            dma((128,)), dma((128,)), dma((1,)), dma((4,)),
         ],
         compiler_params=pltpu.CompilerParams(
             has_side_effects=True, collective_id=0, vmem_limit_bytes=63 << 20),

time: 81 us -> 81 us (level)
  no operation moved by 1% of the time
where the time goes in v7:
time: 81 us; the launch traced here: 80.8 us
  Pallas kernels  79.4 us (98%)
  local copies, waits for them, and re-layouts  1.38 us (2%)
    pallas_call x1, Pallas kernels, shards(): pl.pallas_call(kernel, out_shape=jax.ShapeDtypeStruct((64, 128), F32), in...  79.4 us

profile of v7, /device:TPU:1, one launch (start us, length us, event | category | flops | bytes accessed | tf_op | source)
XLA Modules:
  0.0 80.8 jit_solution(14274820555042357198)
XLA Ops:
  0.0 79.4 %shard_map.64 = f32[64,128]{1,0:T(8,128)} custom-call(s32[8,16]{1,0:T(8,128)} %bitcast.3, s32[16]{0:T(128)} %owner_in.1, s32[16]{0:T(128)} %sizes_in.1, bf16[128,32,256]{2,1,0:T(8,128)(2,1)} %ints.1, bf16[32,512]{1,0:T(8,128)(2,1)} %virt.1, bf16[32,512]{1,0:T(8,128)(2,1)} %occ.1), custom_call_target="tpu_custom_call" | custom-call | tf_op jit(solution)/shard_map/pallas_call | solution.py:330
  79.4 1.4 %copy.8 = f32[128,64]{0,1:T(8,128)} copy(f32[128,64]{0,1:T(8,128)} %bitcast.2) | data formatting | bytes 65536
